TPU v7x, 256 devices: a whole 4x4x8 slice. The times are simulated.
256 devices in a mesh: blk: 64 (over y_lo, z, x), row: 4 (over y_hi, core).
Axes of the slice: x: 4, y: 4 (y_hi: 2, y_lo: 2; y = y_hi * 2 + y_lo), z: 8, core: 2. Of those that a mesh axis runs over, the one named last changes fastest.
Arguments:
- transmission: float32 [16384, 2, 8192], P(('blk', 'row')), may hold values from -64 to 64, as said below
- assignment: int32 [256], replicated, may hold values from 0 to 255, each once
- pairing: int32 [2, 64], replicated, may hold values from 0 to 2
Outputs:
- rotated: float32 [16384, 2, 8192], P(('blk', 'row'))
Inputs may be any that keep to these rules, and one draw needn't show every extreme that they name: `transmission`: entries are real and imaginary parts of a measured speckle field; columns and rows have differing gains. `assignment`: A permutation of the block numbers.
All inputs are finite; a program needn't handle non-finite values.
Results may differ from a plain program's by a relative error of at most 0.00016.
Values sent between devices are 32-bit elements; how exact they have to be, the bound alone decides.
A program may use at most 128 MiB of HBM per device.

v0:
```python
import jax
import jax.numpy as jnp
from jax import lax
from jax.sharding import PartitionSpec as P

ROWS = 16384
BLOCK = 32
SLOTS = 4
ROUNDS = 2
NS_STEPS = 6


def shifted(block, axis, distance):
    devices = range(lax.axis_size(axis))
    route = [((i - distance) % len(devices), i) for i in devices]
    return lax.ppermute(block, axis, route)


def kernel_rotation(real_part, imag_part):
    kernel = jnp.concatenate(
        [
            jnp.concatenate([real_part, imag_part], axis=1),
            jnp.concatenate([-imag_part, real_part], axis=1),
        ],
        axis=0,
    )
    scale = jnp.sqrt(jnp.sum(kernel * kernel))
    eye = jnp.eye(kernel.shape[0], dtype=jnp.float32)
    upper = kernel / scale
    lower = eye
    for step in range(NS_STEPS):
        middle = 1.5 * eye - 0.5 * jnp.dot(lower, upper, precision=lax.Precision.HIGHEST)
        upper = jnp.dot(upper, middle, precision=lax.Precision.HIGHEST)
        lower = jnp.dot(middle, lower, precision=lax.Precision.HIGHEST)
    return lower * jnp.sqrt(ROWS / scale)


def pair_rotation(gram):
    half = gram.shape[0] // 2
    real_part = gram[:half, :half] + gram[half:, half:]
    imag_part = gram[:half, half:] - gram[half:, :half]
    return kernel_rotation(real_part, imag_part)


def local_gram(joined):
    return jnp.dot(joined.T, joined, precision=lax.Precision.HIGHEST)


def summed_pair(joined):
    gram = lax.psum(local_gram(joined), "row")
    return jnp.dot(joined, pair_rotation(gram), precision=lax.Precision.HIGHEST)


def column_index(held, total_cols):
    parts = jnp.arange(2, dtype=jnp.int32)[None, :, None, None] * total_cols
    starts = held[:, None, :, None] * BLOCK
    within = jnp.arange(BLOCK, dtype=jnp.int32)[None, None, None, :]
    return (parts + starts + within).reshape(-1)


def slot_columns(slots):
    parts = jnp.arange(2, dtype=jnp.int32)[:, None, None] * (SLOTS * BLOCK)
    starts = slots[None, :, None] * BLOCK
    within = jnp.arange(BLOCK, dtype=jnp.int32)[None, None, :]
    return (parts + starts + within).reshape(-1)


def inverse_of(index):
    return (
        jnp.zeros(index.shape, jnp.int32).at[index].set(jnp.arange(index.shape[0], dtype=jnp.int32))
    )


def turn_held(held):
    return jnp.stack(
        [held[:, 0], jnp.roll(held[:, 1], 1), jnp.roll(held[:, 2], -1), held[:, 3]], axis=1
    )


def on_device(transmission, assignment, pairing):
    nblk = lax.axis_size("blk")
    me_blk = lax.axis_index("blk")
    row_part = transmission.shape[0]
    total_cols = transmission.shape[2]
    orders = jnp.array([[0, 1, 2, 3], [0, 2, 1, 3], [0, 3, 1, 2]], dtype=jnp.int32)
    held = assignment.reshape(nblk, SLOTS)
    flat = transmission.reshape(row_part, 2 * total_cols)
    outgoing = jnp.take(flat, column_index(held, total_cols), axis=1)
    blocks = lax.all_to_all(outgoing, "blk", split_axis=1, concat_axis=0, tiled=True)
    owned_rows = blocks.shape[0]
    for rnd in range(ROUNDS):
        pick = pairing[rnd, me_blk]
        order = orders[pick]
        first_cols = slot_columns(order[0:2])
        second_cols = slot_columns(order[2:4])
        first = jnp.take(blocks, first_cols, axis=1)
        second = jnp.take(blocks, second_cols, axis=1)
        new_first = summed_pair(first)
        new_second = summed_pair(second)
        joined = jnp.concatenate([new_first, new_second], axis=1)
        back = inverse_of(jnp.concatenate([first_cols, second_cols]))
        blocks = jnp.take(joined, back, axis=1)
        if rnd < ROUNDS - 1:
            lanes = owned_rows * 2 * BLOCK // 128
            up_cols = slot_columns(jnp.array([1], dtype=jnp.int32))
            down_cols = slot_columns(jnp.array([2], dtype=jnp.int32))
            moved_up = shifted(jnp.take(blocks, up_cols, axis=1).reshape(lanes, 128), "blk", 1)
            moved_down = shifted(jnp.take(blocks, down_cols, axis=1).reshape(lanes, 128), "blk", -1)
            blocks = blocks.at[:, up_cols].set(moved_up.reshape(owned_rows, 2 * BLOCK))
            blocks = blocks.at[:, down_cols].set(moved_down.reshape(owned_rows, 2 * BLOCK))
            held = turn_held(held)
    returned = lax.all_to_all(blocks, "blk", split_axis=0, concat_axis=1, tiled=True)
    placed = column_index(held, total_cols)
    rotated = jnp.take(returned, inverse_of(placed), axis=1)
    return rotated.reshape(row_part, 2, total_cols)


def solution(mesh):
    placed = (P(("blk", "row"), None, None), P(), P())
    return jax.shard_map(
        on_device,
        mesh=mesh,
        in_specs=placed,
        out_specs=P(("blk", "row"), None, None),
        check_vma=False,
    )
```

profile of v0, /device:TPU:6, one launch (start us, length us, event | category | flops | bytes accessed | tf_op | source)
XLA Modules:
  0.0 666.9 jit_solution(6179644993815325899)
XLA Ops:
  10.4 8.4 %copy.43 = f32[64,2,8192]{0,2,1:T(8,128)} copy(f32[64,2,8192]{2,1,0:T(2,128)} %param.14) | data formatting | bytes 8388608 | tf_op args[0]
  18.8 58.2 %gather_fusion = f32[16384,64]{1,0:T(8,128)} fusion(f32[64,16384]{0,1:T(8,128)} %bitcast.203, s32[16384]{0:T(1024)S(1)} %fusion.68), kind=kCustom, calls=%fused_computation.clone | custom fusion | bytes 8454144 | tf_op jit(solution)/shard_map/jit(_take)/gather | solution.py:88
  77.0 13.1 %broadcast_select_fusion.1 = f32[16384,64]{1,0:T(8,128)} fusion(f32[16384,64]{1,0:T(8,128)} %gather_fusion, pred[16384]{0:T(1024)(128)(4,1)S(1)} %compare_and_fusion.1), kind=kLoop, calls=%fused_computation.20 | loop fusion | flops 1048576 | bytes 8404992 | tf_op jit(solution)/shard_map/jit(_take)/select_n | solution.py:88
  90.1 6.8 %copy.44 = f32[64,64,256]{2,0,1:T(8,128)} copy(f32[64,64,256]{0,2,1:T(8,128)} %bitcast.204) | data formatting | bytes 8388608 | tf_op jit(solution)/shard_map/all_to_all | solution.py:89
  96.9 13.3 %all-to-all-start = ((f32[64,64,256]{2,0,1:T(8,128)}), f32[64,64,256]{2,0,1:T(8,128)}, u32[]{:S(2)}, u32[]{:S(2)}) async-start(f32[64,64,256]{2,0,1:T(8,128)} %copy.44), calls=%async_computation | async-start | bytes 8388608 | tf_op jit(solution)/shard_map/all_to_all | solution.py:89
  117.8 87.9 %all-to-all-done = f32[64,64,256]{2,0,1:T(8,128)} async-done(((f32[64,64,256]{2,0,1:T(8,128)}), f32[64,64,256]{2,0,1:T(8,128)}, u32[]{:S(2)}, u32[]{:S(2)}) %all-to-all-start) | async-done | bytes 4194336 | tf_op jit(solution)/shard_map/all_to_all | solution.py:89
  205.7 5.6 copy.45
  211.3 5.6 gather_fusion.2
  231.0 40.0 %all-reduce.7.cloned.1.call-done = (f32[128,128]{1,0:T(8,128)}, f32[128,128]{1,0:T(8,128)}) async-done(((f32[128,128]{1,0:T(8,128)}, f32[128,128]{1,0:T(8,128)}), (f32[128,128]{1,0:T(8,128)}, f32[128,128]{1,0:T(8,128)})) %all-reduce.7.cloned.1.call-update) | async-done | bytes 131088 | tf_op jit(solution)/shard_map/psum | solution.py:50
  292.1 7.8 %gather_fusion.3 = f32[256,4096]{1,0:T(8,128)} fusion(f32[4096,256]{0,1:T(8,128)} %pad_maximum_fusion, s32[1024]{0:T(1024)S(1)} %pad_clamp_fusion.5), kind=kCustom, calls=%fused_computation.2.clone | custom fusion | bytes 8389632 | tf_op jit(solution)/shard_map/jit(_take)/gather | solution.py:102
  320.7 21.5 %collective-permute-done = f32[2048,128]{1,0:T(8,128)} collective-permute-done((f32[2048,128]{1,0:T(8,128)}, f32[2048,128]{1,0:T(8,128)}, u32[]{:S(2)}, u32[]{:S(2)}) %collective-permute-start) | collective-permute-done | bytes 1048608 | tf_op jit(solution)/shard_map/ppermute | solution.py:16
  352.6 5.3 scatter_fusion
  357.9 5.5 scatter_fusion.1
  363.4 5.6 gather_fusion.7
  381.1 44.9 %all-reduce.5.cloned.1.call-done = (f32[128,128]{1,0:T(8,128)}, f32[128,128]{1,0:T(8,128)}) async-done(((f32[128,128]{1,0:T(8,128)}, f32[128,128]{1,0:T(8,128)}), (f32[128,128]{1,0:T(8,128)}, f32[128,128]{1,0:T(8,128)})) %all-reduce.5.cloned.1.call-update) | async-done | bytes 131088 | tf_op jit(solution)/shard_map/psum | solution.py:50
  447.3 7.8 %gather_fusion.8 = f32[256,4096]{1,0:T(8,128)} fusion(f32[4096,256]{0,1:T(8,128)} %pad_maximum_fusion.1, s32[1024]{0:T(1024)S(1)} %pad_clamp_fusion), kind=kCustom, calls=%fused_computation.8.clone | custom fusion | bytes 8389632 | tf_op jit(solution)/shard_map/jit(_take)/gather | solution.py:102
  459.9 5.6 copy.51
  465.5 10.7 %all-to-all-start.1 = ((f32[64,64,256]{2,1,0:T(8,128)}), f32[64,64,256]{2,1,0:T(8,128)}, u32[]{:S(2)}, u32[]{:S(2)}) async-start(f32[64,64,256]{2,1,0:T(8,128)} %bitcast.206), calls=%async_computation.1 | async-start | bytes 8388608 | tf_op jit(solution)/shard_map/all_to_all | solution.py:112
  476.8 60.3 %scatter_custom_fusion.4 = s32[16384]{0:T(1024)S(1)} fusion(s32[16384]{0:T(1024)S(1)} %bitcast.209, s32[16384]{0:T(1024)S(1)} %iota.215, s32[]{:T(128)} %constant.15.clone.1), kind=kCustom, calls=%fused_computation.148 | custom fusion | bytes 65540 | tf_op jit(solution)/shard_map/scatter | solution.py:70
  537.2 35.8 %all-to-all-done.1 = f32[64,64,256]{2,1,0:T(8,128)} async-done(((f32[64,64,256]{2,1,0:T(8,128)}), f32[64,64,256]{2,1,0:T(8,128)}, u32[]{:S(2)}, u32[]{:S(2)}) %all-to-all-start.1) | async-done | bytes 4194336 | tf_op jit(solution)/shard_map/all_to_all | solution.py:112
  573.0 6.9 %copy.52 = f32[64,64,256]{0,2,1:T(8,128)} copy(f32[64,64,256]{2,0,1:T(8,128)} %bitcast.32) | data formatting | bytes 8388608 | tf_op jit(solution)/shard_map/all_to_all | solution.py:112
  579.9 58.2 %gather_fusion.9 = f32[16384,64]{1,0:T(8,128)} fusion(f32[64,16384]{0,1:T(8,128)} %bitcast.202, s32[16384]{0:T(1024)S(1)} %fusion.69), kind=kCustom, calls=%fused_computation.4.clone | custom fusion | bytes 8454144 | tf_op jit(solution)/shard_map/jit(_take)/gather | solution.py:114
  638.1 13.1 %broadcast_select_fusion = f32[16384,64]{1,0:T(8,128)} fusion(f32[16384,64]{1,0:T(8,128)} %gather_fusion.9, pred[16384]{0:T(1024)(128)(4,1)S(1)} %compare_and_fusion), kind=kLoop, calls=%fused_computation.19 | loop fusion | flops 1048576 | bytes 8404992 | tf_op jit(solution)/shard_map/jit(_take)/select_n | solution.py:114
  651.2 8.6 %copy.53 = f32[64,2,8192]{2,1,0:T(2,128)} copy(f32[64,2,8192]{0,2,1:T(8,128)} %bitcast.205) | data formatting | bytes 8388608 | tf_op jit(solution)/shard_map/reshape | solution.py:115
  (199 shorter events, 108.7 us)
Async XLA Ops:
  96.9 13.4 %copy-start.4 = (s32[2,64]{1,0:T(2,128)S(1)}, s32[2,64]{1,0:T(2,128)}, u32[]{:S(2)}) copy-start(s32[2,64]{1,0:T(2,128)} %param.16) | copy-start | bytes 1540
  96.9 17.8 %copy-start.5 = (s32[3,4]{1,0:T(4,128)S(1)}, s32[3,4]{1,0:T(4,128)}, u32[]{:S(2)}) copy-start(s32[3,4]{1,0:T(4,128)} %constant.22.clone) | copy-start | bytes 148
  96.9 108.8 %all-to-all-start = ((f32[64,64,256]{2,0,1:T(8,128)}), f32[64,64,256]{2,0,1:T(8,128)}, u32[]{:S(2)}, u32[]{:S(2)}) async-start(f32[64,64,256]{2,0,1:T(8,128)} %copy.44), calls=%async_computation | async-start | bytes 8388608 | tf_op jit(solution)/shard_map/all_to_all | solution.py:89
  110.2 160.8 %all-reduce.7.cloned.1.call-start = ((), (), s32[]{:S(2)}) async-start(), calls=%async_computation.3 | async-start | bytes 262144 | tf_op jit(solution)/shard_map/psum | solution.py:50
  228.9 197.0 %all-reduce.5.cloned.1.call-start = ((), (), s32[]{:S(2)}) async-start(), calls=%async_computation.2 | async-start | bytes 262144 | tf_op jit(solution)/shard_map/psum | solution.py:50
  271.0 5.6 copy-start.2
  287.4 2.2 copy-start
  316.6 25.7 %collective-permute-start = (f32[2048,128]{1,0:T(8,128)}, f32[2048,128]{1,0:T(8,128)}, u32[]{:S(2)}, u32[]{:S(2)}) collective-permute-start(f32[2048,128]{1,0:T(8,128)} %reshape.609), channel_id=1, source_target_pairs={{252,0},{0,4},{4,8},{8,12},{12,16},{16,20},{20,24},{24,28},{28,32}... | collective-permute-start | bytes 3145736 | tf_op jit(solution)/shard_map/ppermute | solution.py:16
  320.2 27.5 %collective-permute-start.1 = (f32[2048,128]{1,0:T(8,128)}, f32[2048,128]{1,0:T(8,128)}, u32[]{:S(2)}, u32[]{:S(2)}) collective-permute-start(f32[2048,128]{1,0:T(8,128)} %reshape.611), channel_id=1, source_target_pairs={{4,0},{8,4},{12,8},{16,12},{20,16},{24,20},{28,24},{32,28},{36,32}... | collective-permute-start | bytes 3145736 | tf_op jit(solution)/shard_map/ppermute | solution.py:16
  425.9 5.6 copy-start.3
  442.6 2.2 copy-start.1
  465.5 107.5 %all-to-all-start.1 = ((f32[64,64,256]{2,1,0:T(8,128)}), f32[64,64,256]{2,1,0:T(8,128)}, u32[]{:S(2)}, u32[]{:S(2)}) async-start(f32[64,64,256]{2,1,0:T(8,128)} %bitcast.206), calls=%async_computation.1 | async-start | bytes 8388608 | tf_op jit(solution)/shard_map/all_to_all | solution.py:112
Sparse Core Ops, SparseCore 0:
  229.0 41.9 all-reduce.6
  381.2 44.7 all-reduce.4
where the time goes:
time: 673 us; the launch traced here: 667 us
  local copies, waits for them, and re-layouts  292 us (43%)
  waiting for transfers between devices  233 us (35%)
  other arithmetic  49.8 us (7%)
  matrix products  44.1 us (7%)
  starting transfers between devices  26.1 us (4%)
  between operations  21.6 us (3%)
    all_to_all x1, waiting for transfers between devices, on_device(): lax.all_to_all(outgoing, 'blk', split_axis=1, concat_axis=0, tiled=True)  87.9 us
    psum x2, waiting for transfers between devices, summed_pair(): gram = lax.psum(local_gram(joined), 'row')  84.8 us
    scatter x3, local copies, waits for them, and re-layouts, inverse_of(): jnp.zeros(index.shape, jnp.int32).at[index]  63.5 us
    gather x1, local copies, waits for them, and re-layouts, on_device(): outgoing = jnp.take(flat, column_index(held, total_cols), axis=1)  58.2 us
    gather x1, local copies, waits for them, and re-layouts, on_device(): rotated = jnp.take(returned, inverse_of(placed), axis=1)  58.2 us
    all_to_all x1, waiting for transfers between devices, on_device(): lax.all_to_all(blocks, 'blk', split_axis=0, concat_axis=1, tiled=True)  35.8 us
    ppermute x2, waiting for transfers between devices, shifted(): return lax.ppermute(block, axis, route)  24.8 us
    gather x2, local copies, waits for them, and re-layouts, on_device(): blocks = jnp.take(joined, back, axis=1)  15.6 us
  transfers between devices with their start and end apart: 6, of which 6 were waited for; matrix products, arithmetic and copies ran while one was open for 11% of the time, Pallas kernels for 0%

commit v1 on v0

--- a/solution.py
+++ b/solution.py
@@ -47,7 +47,9 @@
 
 
 def summed_pair(joined):
-    gram = lax.psum(local_gram(joined), "row")
+    block_2 = local_gram(joined)
+    pieces = lax.all_gather(block_2, "row")
+    gram = jnp.sum(pieces, axis=0)
     return jnp.dot(joined, pair_rotation(gram), precision=lax.Precision.HIGHEST)
 
 

time: 673 us -> 610 us (0.906)
  waiting for transfers between devices: 233 us -> 146 us
  blocking collectives: 0 us -> 30.1 us
  between operations: 21.6 us -> 8.42 us
  local copies, waits for them, and re-layouts: 292 us -> 302 us
    psum x2 -> x0, waiting for transfers between devices: 84.8 us -> none  [summed_pair(): gram = lax.psum(local_gram(joined), 'row')]
    all_gather x0 -> x4, blocking collectives: none -> 30.1 us  [summed_pair(): pieces = lax.all_gather(block_2, 'row')]
    gather x1, local copies, waits for them, and re-layouts: 3.57 us -> 15.4 us  [on_device(): jnp.take(blocks, up_cols, axis=1).reshape(lanes, 128)]
  transfers between devices with their start and end apart: 6 -> 4, of which waited for: 6 -> 4; matrix products, arithmetic and copies ran while one was open for 11% -> 12% of each run, Pallas kernels for 0% -> 0%
where the time goes in v1:
time: 610 us; the launch traced here: 602 us
  local copies, waits for them, and re-layouts  302 us (50%)
  waiting for transfers between devices  146 us (24%)
  other arithmetic  48.1 us (8%)
  matrix products  41.6 us (7%)
  blocking collectives  30.1 us (5%)
  starting transfers between devices  25.6 us (4%)
  between operations  8.42 us (1%)
    all_to_all x1, waiting for transfers between devices, on_device(): lax.all_to_all(outgoing, 'blk', split_axis=1, concat_axis=0, tiled=True)  88 us
    scatter x3, local copies, waits for them, and re-layouts, inverse_of(): jnp.zeros(index.shape, jnp.int32).at[index]  63.1 us
    gather x1, local copies, waits for them, and re-layouts, on_device(): outgoing = jnp.take(flat, column_index(held, total_cols), axis=1)  57.8 us
    gather x1, local copies, waits for them, and re-layouts, on_device(): rotated = jnp.take(returned, inverse_of(placed), axis=1)  57.8 us
    all_to_all x1, waiting for transfers between devices, on_device(): lax.all_to_all(blocks, 'blk', split_axis=0, concat_axis=1, tiled=True)  35.6 us
    all_gather x4, blocking collectives, summed_pair(): pieces = lax.all_gather(block_2, 'row')  30.1 us
    ppermute x2, waiting for transfers between devices, shifted(): return lax.ppermute(block, axis, route)  21.9 us
    gather x2, local copies, waits for them, and re-layouts, on_device(): blocks = jnp.take(joined, back, axis=1)  15.6 us
  transfers between devices with their start and end apart: 4, of which 4 were waited for; matrix products, arithmetic and copies ran while one was open for 12% of the time, Pallas kernels for 0%

profile of v1, /device:TPU:6, one launch (start us, length us, event | category | flops | bytes accessed | tf_op | source)
XLA Modules:
  0.0 601.5 jit_solution(1130503070791111704)
XLA Ops:
  4.0 8.3 %copy.58 = f32[64,2,8192]{0,2,1:T(8,128)} copy(f32[64,2,8192]{2,1,0:T(2,128)} %param.14) | data formatting | bytes 8388608 | tf_op args[0]
  12.3 57.8 %gather_fusion = f32[16384,64]{1,0:T(8,128)} fusion(f32[64,16384]{0,1:T(8,128)} %bitcast.207, s32[16384]{0:T(1024)S(1)} %fusion.68), kind=kCustom, calls=%fused_computation.clone | custom fusion | bytes 8454144 | tf_op jit(solution)/shard_map/jit(_take)/gather | solution.py:90
  70.0 13.1 %broadcast_select_fusion.1 = f32[16384,64]{1,0:T(8,128)} fusion(f32[16384,64]{1,0:T(8,128)} %gather_fusion, pred[16384]{0:T(1024)(128)(4,1)S(1)} %compare_and_fusion.1), kind=kLoop, calls=%fused_computation.20 | loop fusion | flops 1048576 | bytes 8404992 | tf_op jit(solution)/shard_map/jit(_take)/select_n | solution.py:90
  83.2 6.8 %copy.59 = f32[64,64,256]{2,0,1:T(8,128)} copy(f32[64,64,256]{0,2,1:T(8,128)} %bitcast.208) | data formatting | bytes 8388608 | tf_op jit(solution)/shard_map/all_to_all | solution.py:91
  89.9 13.3 %all-to-all-start = ((f32[64,64,256]{2,0,1:T(8,128)}), f32[64,64,256]{2,0,1:T(8,128)}, u32[]{:S(2)}, u32[]{:S(2)}) async-start(f32[64,64,256]{2,0,1:T(8,128)} %copy.59), calls=%async_computation | async-start | bytes 8388608 | tf_op jit(solution)/shard_map/all_to_all | solution.py:91
  110.8 88.0 %all-to-all-done = f32[64,64,256]{2,0,1:T(8,128)} async-done(((f32[64,64,256]{2,0,1:T(8,128)}), f32[64,64,256]{2,0,1:T(8,128)}, u32[]{:S(2)}, u32[]{:S(2)}) %all-to-all-start) | async-done | bytes 4194336 | tf_op jit(solution)/shard_map/all_to_all | solution.py:91
  210.8 7.5 %all-gather.1 = f32[512,128]{1,0:T(8,128)S(1)} all-gather(f32[128,128]{1,0:T(8,128)S(1)} %fusion.10), channel_id=3, replica_groups=mesh['blk'=64,'row'=4] {'row'}, dimensions={0}, use_global_device_ids=true | all-gather | bytes 327680 | tf_op jit(solution)/shard_map/all_gather | solution.py:51
  223.2 5.7 gather_fusion.1
  233.1 7.7 %all-gather = f32[512,128]{1,0:T(8,128)S(1)} all-gather(f32[128,128]{1,0:T(8,128)S(1)} %fusion.14), channel_id=2, replica_groups=mesh['blk'=64,'row'=4] {'row'}, dimensions={0}, use_global_device_ids=true | all-gather | bytes 327680 | tf_op jit(solution)/shard_map/all_gather | solution.py:51
  256.5 7.8 %gather_fusion.3 = f32[256,4096]{1,0:T(8,128)} fusion(f32[4096,256]{0,1:T(8,128)} %pad_maximum_fusion, s32[1024]{0:T(1024)S(1)} %pad_clamp_fusion.5), kind=kCustom, calls=%fused_computation.2.clone | custom fusion | bytes 8389632 | tf_op jit(solution)/shard_map/jit(_take)/gather | solution.py:104
  272.7 15.4 %gather_fusion.4 = f32[64,4096]{1,0:T(8,128)S(1)} fusion(f32[4096,256]{0,1:T(8,128)} %select_bitcast_fusion.1, s32[1024]{0:T(1024)S(1)} %get-tuple-element.62), kind=kCustom, calls=%fused_computation.3.clone | custom fusion | bytes 2097408 | tf_op jit(solution)/shard_map/jit(_take)/gather | solution.py:109
  298.2 19.9 %collective-permute-done = f32[2048,128]{1,0:T(8,128)} collective-permute-done((f32[2048,128]{1,0:T(8,128)}, f32[2048,128]{1,0:T(8,128)}, u32[]{:S(2)}, u32[]{:S(2)}) %collective-permute-start) | collective-permute-done | bytes 1048608 | tf_op jit(solution)/shard_map/ppermute | solution.py:16
  344.3 7.3 %all-gather.3 = f32[512,128]{1,0:T(8,128)S(1)} all-gather(f32[128,128]{1,0:T(8,128)S(1)} %fusion.2), channel_id=5, replica_groups=mesh['blk'=64,'row'=4] {'row'}, dimensions={0}, use_global_device_ids=true | all-gather | bytes 327680 | tf_op jit(solution)/shard_map/all_gather | solution.py:51
  356.5 5.7 gather_fusion.6
  366.5 7.6 %all-gather.2 = f32[512,128]{1,0:T(8,128)S(1)} all-gather(f32[128,128]{1,0:T(8,128)S(1)} %fusion.6), channel_id=4, replica_groups=mesh['blk'=64,'row'=4] {'row'}, dimensions={0}, use_global_device_ids=true | all-gather | bytes 327680 | tf_op jit(solution)/shard_map/all_gather | solution.py:51
  389.7 7.8 %gather_fusion.8 = f32[256,4096]{1,0:T(8,128)} fusion(f32[4096,256]{0,1:T(8,128)} %pad_maximum_fusion.1, s32[1024]{0:T(1024)S(1)} %pad_clamp_fusion), kind=kCustom, calls=%fused_computation.8.clone | custom fusion | bytes 8389632 | tf_op jit(solution)/shard_map/jit(_take)/gather | solution.py:104
  402.3 5.6 copy.66
  407.9 10.3 %all-to-all-start.1 = ((f32[64,64,256]{2,1,0:T(8,128)}), f32[64,64,256]{2,1,0:T(8,128)}, u32[]{:S(2)}, u32[]{:S(2)}) async-start(f32[64,64,256]{2,1,0:T(8,128)} %bitcast.210), calls=%async_computation.1 | async-start | bytes 8388608 | tf_op jit(solution)/shard_map/all_to_all | solution.py:114
  418.7 60.3 %scatter_custom_fusion.4 = s32[16384]{0:T(1024)S(1)} fusion(s32[16384]{0:T(1024)S(1)} %bitcast.217, s32[16384]{0:T(1024)S(1)} %iota.215, s32[]{:T(128)} %constant.15.clone.1), kind=kCustom, calls=%fused_computation.148 | custom fusion | bytes 65540 | tf_op jit(solution)/shard_map/scatter | solution.py:72
  479.1 35.6 %all-to-all-done.1 = f32[64,64,256]{2,1,0:T(8,128)} async-done(((f32[64,64,256]{2,1,0:T(8,128)}), f32[64,64,256]{2,1,0:T(8,128)}, u32[]{:S(2)}, u32[]{:S(2)}) %all-to-all-start.1) | async-done | bytes 4194336 | tf_op jit(solution)/shard_map/all_to_all | solution.py:114
  514.7 6.9 %copy.67 = f32[64,64,256]{0,2,1:T(8,128)} copy(f32[64,64,256]{2,0,1:T(8,128)} %bitcast.36) | data formatting | bytes 8388608 | tf_op jit(solution)/shard_map/all_to_all | solution.py:114
  521.6 57.8 %gather_fusion.9 = f32[16384,64]{1,0:T(8,128)} fusion(f32[64,16384]{0,1:T(8,128)} %bitcast.206, s32[16384]{0:T(1024)S(1)} %fusion.69), kind=kCustom, calls=%fused_computation.4.clone | custom fusion | bytes 8454144 | tf_op jit(solution)/shard_map/jit(_take)/gather | solution.py:116
  579.4 13.1 %broadcast_select_fusion = f32[16384,64]{1,0:T(8,128)} fusion(f32[16384,64]{1,0:T(8,128)} %gather_fusion.9, pred[16384]{0:T(1024)(128)(4,1)S(1)} %compare_and_fusion), kind=kLoop, calls=%fused_computation.19 | loop fusion | flops 1048576 | bytes 8404992 | tf_op jit(solution)/shard_map/jit(_take)/select_n | solution.py:116
  592.5 8.6 %copy.68 = f32[64,2,8192]{2,1,0:T(2,128)} copy(f32[64,2,8192]{0,2,1:T(8,128)} %bitcast.209) | data formatting | bytes 8388608 | tf_op jit(solution)/shard_map/reshape | solution.py:117
  (197 shorter events, 115.4 us)
Async XLA Ops:
  89.9 13.3 %copy-start.2 = (s32[2,64]{1,0:T(2,128)S(1)}, s32[2,64]{1,0:T(2,128)}, u32[]{:S(2)}) copy-start(s32[2,64]{1,0:T(2,128)} %param.16) | copy-start | bytes 1540
  89.9 17.6 %copy-start.3 = (s32[3,4]{1,0:T(4,128)S(1)}, s32[3,4]{1,0:T(4,128)}, u32[]{:S(2)}) copy-start(s32[3,4]{1,0:T(4,128)} %constant.22.clone) | copy-start | bytes 148
  89.9 108.8 %all-to-all-start = ((f32[64,64,256]{2,0,1:T(8,128)}), f32[64,64,256]{2,0,1:T(8,128)}, u32[]{:S(2)}, u32[]{:S(2)}) async-start(f32[64,64,256]{2,0,1:T(8,128)} %copy.59), calls=%async_computation | async-start | bytes 8388608 | tf_op jit(solution)/shard_map/all_to_all | solution.py:91
  250.1 3.9 copy-start
  292.4 25.7 %collective-permute-start = (f32[2048,128]{1,0:T(8,128)}, f32[2048,128]{1,0:T(8,128)}, u32[]{:S(2)}, u32[]{:S(2)}) collective-permute-start(f32[2048,128]{1,0:T(8,128)} %reshape.609), channel_id=1, source_target_pairs={{252,0},{0,4},{4,8},{8,12},{12,16},{16,20},{20,24},{24,28},{28,32}... | collective-permute-start | bytes 3145736 | tf_op jit(solution)/shard_map/ppermute | solution.py:16
  294.5 27.8 %collective-permute-start.1 = (f32[2048,128]{1,0:T(8,128)}, f32[2048,128]{1,0:T(8,128)}, u32[]{:S(2)}, u32[]{:S(2)}) collective-permute-start(f32[2048,128]{1,0:T(8,128)} %reshape.611), channel_id=1, source_target_pairs={{4,0},{8,4},{12,8},{16,12},{20,16},{24,20},{28,24},{32,28},{36,32}... | collective-permute-start | bytes 3145736 | tf_op jit(solution)/shard_map/ppermute | solution.py:16
  383.3 3.9 copy-start.1
  407.9 106.9 %all-to-all-start.1 = ((f32[64,64,256]{2,1,0:T(8,128)}), f32[64,64,256]{2,1,0:T(8,128)}, u32[]{:S(2)}, u32[]{:S(2)}) async-start(f32[64,64,256]{2,1,0:T(8,128)} %bitcast.210), calls=%async_computation.1 | async-start | bytes 8388608 | tf_op jit(solution)/shard_map/all_to_all | solution.py:114
